TPU v7x, 32 devices: a whole 2x2x4 slice. The times are simulated.
32 devices in a mesh: dp: 8 (over z, y), tensor: 4 (over x, core).
Axes of the slice: x: 2, y: 2, z: 4, core: 2. Of those that a mesh axis runs over, the one named last changes fastest.
Arguments:
- tokens: bfloat16 [8192, 1536], P('dp'), may hold values from -6 to 6
- inproj: bfloat16 [2, 2, 1536, 3072], P(None, None, 'dp', 'tensor'), may hold values from -0.15625 to 0.15625
- stepproj: bfloat16 [2, 1536, 48], P(None, None, 'tensor'), may hold values from -0.15625 to 0.15625
- stateproj: bfloat16 [2, 1536, 256], replicated, may hold values from -0.15625 to 0.15625
- outproj: bfloat16 [2, 3072, 1536], P(None, 'tensor', 'dp'), may hold values from -0.109375 to 0.109375
- convinner: float32 [2, 4, 3072], P(None, None, 'tensor'), may hold values from -3 to 3
- biasinner: float32 [2, 3072], P(None, 'tensor'), may hold values from -0.5 to 0.5
- convstate: float32 [2, 4, 256], replicated, may hold values from -3 to 3
- biasstate: float32 [2, 256], replicated, may hold values from -0.5 to 0.5
- stepbias: float32 [2, 48], P(None, 'tensor'), may hold values from -6 to -3
- decaylog: float32 [2, 48], P(None, 'tensor'), may hold values from 0 to 2.77
- skipgain: float32 [2, 48], P(None, 'tensor'), may hold values from 0.5 to 1.5
- normgain: float32 [2, 3072], P(None, 'tensor'), may hold values from 0.5 to 1.5
- inputgain: float32 [2, 1536], replicated, may hold values from 0.5 to 1.5
- cotangent: bfloat16 [8192, 1536], P('dp'), may hold values from -6 to 6
Outputs:
- mixed: bfloat16 [8192, 1536], P('dp')
- grad_tokens: float32 [8192, 1536], P('dp')
- inproj_grad: float32 [2, 2, 1536, 3072], P(None, None, 'dp', 'tensor')
- stepproj_grad: float32 [2, 1536, 48], P(None, None, 'tensor')
- stateproj_grad: float32 [2, 1536, 256], replicated
- outproj_grad: float32 [2, 3072, 1536], P(None, 'tensor', 'dp')
- convinner_grad: float32 [2, 4, 3072], P(None, None, 'tensor')
- biasinner_grad: float32 [2, 3072], P(None, 'tensor')
- convstate_grad: float32 [2, 4, 256], replicated
- biasstate_grad: float32 [2, 256], replicated
- stepbias_grad: float32 [2, 48], P(None, 'tensor')
- decaylog_grad: float32 [2, 48], P(None, 'tensor')
- skipgain_grad: float32 [2, 48], P(None, 'tensor')
- normgain_grad: float32 [2, 3072], P(None, 'tensor')
- inputgain_grad: float32 [2, 1536], replicated
All inputs are finite; a program needn't handle non-finite values.
Results may differ from a plain program's by a relative error of at most 0.02.
Values may be sent and summed in bfloat16 or wider, within the bound.
A program may use at most 256 MiB of HBM per device.

v0:
```python
import functools
import math

import jax
import jax.numpy as jnp
from jax import lax
from jax.experimental import pallas as pl
from jax.experimental.pallas import tpu as pltpu
from jax.sharding import PartitionSpec as P

STATE = 128
LEN = 1024
INNER = 3072
HEAD = 64
CHUNK = 128
SLICE = 256
TILE = 256
PACK = 544
SPAN = 400
VMEM_LIMIT = 65000 * 1024
LANES = 128
EPS = 1e-05
LOG2E = 1.4426950408889634

HIGH = lax.Precision.HIGHEST
NN = (((1,), (0,)), ((), ()))
NT = (((1,), (1,)), ((), ()))
TN = (((0,), (0,)), ((), ()))
F32 = jnp.float32
BF16 = jnp.bfloat16
MESH = pl.DeviceIdType.MESH


def remote(src, dst, send, recv, where):
    return pltpu.make_async_remote_copy(
        src_ref=src, dst_ref=dst, send_sem=send, recv_sem=recv, device_id=where, device_id_type=MESH
    )


class Line:
    def __init__(self, size):
        self.n = size // 2
        me = lax.axis_index("dp")
        self.me = me
        self.at = me // 2
        self.side = lax.rem(me, 2)
        self.pair = {"dp": me + 1 - 2 * self.side}
        self.right = {"dp": jnp.minimum(me + 2, size - 1)}
        self.left = {"dp": jnp.maximum(me - 2, 0)}
        odd = lax.rem(self.at, 2)
        self.odd = odd == 1
        self.near = {"dp": me + 2 - 4 * odd}
        self.has_left = self.at > 0
        self.has_right = self.at < self.n - 1

    def greet(self, barrier, more=()):
        for who in more:
            pl.semaphore_signal(barrier, inc=1, device_id=who, device_id_type=MESH)
        pl.semaphore_signal(barrier, inc=1, device_id=self.pair, device_id_type=MESH)

        @pl.when(self.has_left)
        def _():
            pl.semaphore_signal(barrier, inc=1, device_id=self.left, device_id_type=MESH)

        @pl.when(self.has_right)
        def _():
            pl.semaphore_signal(barrier, inc=1, device_id=self.right, device_id_type=MESH)

        peers = 1 + len(more) + self.has_left.astype(jnp.int32) + self.has_right.astype(jnp.int32)
        pl.semaphore_wait(barrier, peers)

    def greet_all(self, barrier, more=()):
        for who in list(more) + [self.pair]:
            pl.semaphore_signal(barrier, inc=1, device_id=who, device_id_type=MESH)
        for i in range(self.n):
            @pl.when(i != self.at)
            def _(i=i):
                pl.semaphore_signal(barrier, inc=1, device_id={"dp": 2 * i + self.side}, device_id_type=MESH)
        pl.semaphore_wait(barrier, self.n + len(more))


def upper(rows):
    return max(16, rows // 32 * 16)


class Gather:
    def __init__(self, line, own, full, keep, send, recv):
        self.line, self.own, self.full, self.keep, self.send, self.recv = line, own, full, keep, send, recv
        self.rows = full.shape[2]
        self.cut = upper(self.rows)

    def copy(self, j, slab, way, src=None, rest=False):
        where = (self.line.right, self.line.left, self.line.pair)[way]
        dst = self.full.at[j, slab]
        if rest:
            dst = self.full.at[j, slab, pl.ds(self.cut, self.rows - self.cut)]
        return remote(dst if src is None else src, dst, self.send.at[j, way, slab], self.recv.at[j, slab], where)

    def shared(self, j, slab, owner):
        part = self.full.at[j, slab, pl.ds(0, self.cut)]
        return remote(part, part, self.send.at[j, 0, slab], self.recv.at[j, owner], self.line.near)

    def start(self, j):
        line = self.line
        pltpu.make_async_copy(self.own(j), self.full.at[j, line.me], self.keep.at[j]).start()

        @pl.when(line.has_right)
        def _():
            self.copy(j, line.me, 0, self.own(j)).start()

        @pl.when(line.has_left)
        def _():
            self.copy(j, line.me, 1, self.own(j)).start()

        self.copy(j, line.me, 2, self.own(j)).start()

    def relay(self, j, k):
        line = self.line

        def forward(slab, way, go_on, near):
            self.copy(j, slab, way).wait_recv()

            @pl.when(go_on)
            def _():
                self.copy(j, slab, way).start()

            if k > 1:
                self.copy(j, slab, 2).start()
            else:
                @pl.when(near)
                def _():
                    self.copy(j, slab, 2, rest=True).start()

                @pl.when(jnp.logical_not(near))
                def _():
                    self.copy(j, slab, 2).start()

        @pl.when(line.at >= k)
        def _():
            forward(line.me - 2 * k, 0, line.has_right, line.odd)

        @pl.when(line.at + k < line.n)
        def _():
            forward(line.me + 2 * k, 1, line.has_left, jnp.logical_not(line.odd))

        if k == 1:
            slab = line.me + 1 - 2 * line.side
            self.copy(j, slab, 2).wait_recv()
            self.shared(j, slab, line.near["dp"]).start()

    def near_slab(self):
        line = self.line
        return line.near["dp"] + 1 - 2 * line.side

    def arrive(self, j):
        line = self.line
        pltpu.make_async_copy(self.own(j), self.full.at[j, line.me], self.keep.at[j]).wait()
        self.copy(j, self.near_slab(), 2, rest=True).wait_recv()
        self.shared(j, self.near_slab(), line.me).wait_recv()
        for place in range(line.n):
            slab = 2 * place + 1 - line.side

            @pl.when((slab != self.near_slab()) & (place != line.at))
            def _(slab=slab):
                self.copy(j, slab, 2).wait_recv()

    def drain(self, j):
        line = self.line
        self.shared(j, line.me + 1 - 2 * line.side, line.near["dp"]).wait_send()
        for place in range(line.n):
            slab = 2 * place + line.side
            near = slab == line.near["dp"]

            @pl.when(near)
            def _(slab=slab):
                self.copy(j, slab, 2, rest=True).wait_send()

            @pl.when(jnp.logical_not(near))
            def _(slab=slab):
                self.copy(j, slab, 2).wait_send()

            @pl.when(line.has_right & (place <= line.at))
            def _(slab=slab):
                self.copy(j, slab, 0).wait_send()

            @pl.when(line.has_left & (place >= line.at))
            def _(slab=slab):
                self.copy(j, slab, 1).wait_send()


class Square:
    def __init__(self):
        me = lax.axis_index("tensor")
        self.me = me
        self.half = lax.rem(me, 2)
        self.mate = {"tensor": me + 1 - 2 * self.half}
        self.across = {"tensor": lax.rem(me + 2, 4)}

    def others(self):
        return [{"tensor": lax.rem(self.me + k, 4)} for k in (1, 2, 3)]


class Total:
    def __init__(self, square, part, got, far, other, send, recv):
        self.square, self.part, self.got, self.far, self.other = square, part, got, far, other
        self.send, self.recv = send, recv

    def first(self, c):
        sq = self.square
        return remote(
            self.part.at[2 * c + 1 - sq.half], self.got.at[c], self.send.at[0, c], self.recv.at[0, c], sq.mate
        )

    def second(self, c):
        sq = self.square
        return remote(self.part.at[2 * c + sq.half], self.far.at[c], self.send.at[1, c], self.recv.at[1, c], sq.across)

    def third(self, c):
        sq = self.square
        return remote(self.part.at[2 * c + sq.half], self.other.at[c], self.send.at[2, c], self.recv.at[2, c], sq.mate)

    def step(self, kind, c):
        slot = 2 * c + self.square.half
        if kind == 0:
            self.first(c).start()
        elif kind == 1:
            self.first(c).wait_recv()
            self.part[slot] = (self.part[slot].astype(F32) + self.got[c].astype(F32)).astype(BF16)
            self.second(c).start()
        elif kind == 2:
            self.second(c).wait()
            self.part[slot] = (self.part[slot].astype(F32) + self.far[c].astype(F32)).astype(BF16)
            self.third(c).start()
        else:
            self.third(c).wait_recv()
            self.first(c).wait_send()
            self.third(c).wait_send()
            self.part[2 * c + 1 - self.square.half] = self.other[c]


class Scatter:
    def __init__(self, line, part, out, near, far, send, recv):
        self.line, self.part, self.out, self.near, self.far = line, part, out, near, far
        self.send, self.recv = send, recv

    def order(self):
        n = self.line.n
        seq = []
        for i in range((n + 1) // 2):
            seq.append(i)
            if n - 1 - i != i:
                seq.append(n - 1 - i)
        return seq

    def cross(self, j, i):
        line = self.line
        return remote(
            self.part.at[j, 2 * i + 1 - line.side], self.near.at[j, i], self.send.at[0, j, i], self.recv.at[0, j, i], line.pair
        )

    def straight(self, j, i, source):
        line = self.line
        return remote(
            self.part.at[j, 2 * i + line.side], self.far.at[j, source], self.send.at[1, j, i], self.recv.at[1, j, source],
            {"dp": 2 * i + line.side},
        )

    def lead(self, j, m):
        self.cross(j, self.order()[m]).start()

    def start(self, j):
        for m in range(self.line.n):
            self.lead(j, m)

    def emit(self, j, turned, right, now=None):
        rows = self.part.shape[2]
        for m, i in enumerate(self.order()):
            value = mm(turned[2 * i * rows : 2 * (i + 1) * rows, :], right[...]).astype(BF16)
            self.part[j, 2 * i] = value[:rows]
            self.part[j, 2 * i + 1] = value[rows:]
            if now is None or m < now:
                self.lead(j, m)

    def product(self, dst, turned, right):
        rows = dst.shape[1]
        for i in range(self.line.n):
            value = mm(turned[2 * i * rows : 2 * (i + 1) * rows, :], right[...]).astype(BF16)
            dst[2 * i] = value[:rows]
            dst[2 * i + 1] = value[rows:]

    def fold(self, j, m):
        line = self.line
        i = self.order()[m]
        self.cross(j, i).wait_recv()
        slot = 2 * i + line.side
        self.part[j, slot] = (self.part[j, slot].astype(F32) + self.near[j, i].astype(F32)).astype(BF16)

        @pl.when(i != line.at)
        def _():
            self.straight(j, i, line.at).start()

    def finish(self, j):
        line = self.line
        out = self.out(j)
        out[...] = self.part[j, line.me].astype(out.dtype)
        for i in range(line.n):
            @pl.when(i != line.at)
            def _(i=i):
                self.straight(j, i, i).wait_recv()
                out[...] += self.far[j, i].astype(out.dtype)

    def drain(self, j):
        for i in range(self.line.n):
            self.cross(j, i).wait_send()

            @pl.when(i != self.line.at)
            def _(i=i):
                self.straight(j, i, self.line.at).wait_send()


def mm(left, right, dims=NN, precision=None):
    return lax.dot_general(left, right, dims, precision=precision, preferred_element_type=F32)


def sigmoid(v):
    return 0.5 * jnp.tanh(0.5 * v) + 0.5


def softplus(v):
    return jnp.maximum(v, 0.0) + jnp.log1p(jnp.exp(-jnp.abs(v)))


def split16(v):
    top = v.astype(BF16)
    return top, (v - top.astype(F32)).astype(BF16)


def expand(v, ind):
    top, rest = split16(v)
    return mm(top, ind) + mm(rest, ind)


def headsum(v, ind):
    return mm(v.astype(BF16), ind, NT)


def rowsum(v):
    return mm(jnp.ones((8, v.shape[1]), BF16), v.astype(BF16), NT)[0:1, :]


def iotas(n):
    return (
        lax.broadcasted_iota(jnp.int32, (n, n), 0),
        lax.broadcasted_iota(jnp.int32, (n, n), 1),
    )


def colsum(v):
    return jnp.sum(v, axis=0, keepdims=True)


def conv_pre(ext, par, n):
    total = par[4:5, :] + par[0:1, :] * ext[5 : 5 + n, :]
    for tap in range(1, 4):
        total = total + par[tap : tap + 1, :] * ext[5 + tap : 5 + tap + n, :]
    return total


def scan_prep(small, hp, ind, n):
    rows, cols = iotas(n)
    raw = small[:, 2 * STATE :] + hp[0:1, :]
    step = softplus(raw)
    rate = -jnp.exp(hp[1:2, :])
    lower = jnp.where(rows >= cols, 1.0, 0.0).astype(F32)
    cs = mm(lower, step * rate, precision=HIGH)
    tail = jnp.exp(cs[n - 1 : n, :] - cs)
    wide = mm(jnp.concatenate([step, jnp.exp(cs), tail], axis=0).astype(BF16), ind)
    return raw, step, rate, cs, wide[0:n], wide[n : 2 * n], wide[2 * n : 3 * n]


def block_of(slabs, at, rows):
    step = math.gcd(LANES, rows)
    pieces = []
    for k in range(LANES // step):
        row = at * LANES + k * step
        slab = row // rows
        pieces.append(slabs[slab, pl.ds(pl.multiple_of(row - slab * rows, step), step), :])
    return pieces[0] if len(pieces) == 1 else jnp.concatenate(pieces, axis=0)


def put_params(cp, sp, hp, ind, layer, params):
    conv, bias, norm, convs, biass, head = params
    width = cp.shape[1]
    row = lax.broadcasted_iota(jnp.int32, (LANES, width), 0)
    lane = lax.broadcasted_iota(jnp.int32, (LANES, width), 1)
    ind[...] = jnp.where(lane // HEAD == row, 1.0, 0.0).astype(BF16)
    hp[...] = head[layer]
    cp[0:4, :] = conv[layer]
    cp[4:5, :] = bias[layer : layer + 1, :]
    cp[5:6, :] = norm[layer : layer + 1, :]
    cp[6:8, :] = expand(hp[...], ind[...])[2:4, :]
    sp[0:4, :] = convs[layer]
    sp[4:5, :] = biass[layer : layer + 1, :]


def place_rows(dst, at, value):
    r = dst.shape[1]
    for g in range(0, value.shape[0], 16):
        dst[(at + g) // r, (at + g) % r : (at + g) % r + 16, :] = value[g : g + 16].astype(dst.dtype)


def pack_rows(size):
    return -(-PACK // (16 * size)) * 16


def put_pack(dst, me, turned, steps_low, sdel, dcp, dsp, dhp, dgain):
    model = turned.shape[0]
    quarter = model // 4
    w = sdel.shape[1]

    def empty(n):
        return jnp.zeros((n, w), F32)

    place_rows(dst, 0, mm(turned[pl.ds(pl.multiple_of(me * quarter, quarter), quarter), :], sdel[...]))
    place_rows(dst, quarter, jnp.concatenate([dsp, empty(8)], axis=0))
    grown = mm(turned[...], steps_low[...]).T[:16]
    at = quarter + 16
    for b in range(model // w):
        place_rows(dst, at, grown[:, b * w : (b + 1) * w])
        at += 16
    place_rows(dst, at, jnp.concatenate([dcp[:, :w], dcp[:, w : 2 * w]], axis=0))
    place_rows(dst, at + 16, jnp.concatenate([dcp[:, 2 * w :], jnp.concatenate([dhp, dhp], axis=1)], axis=0))
    rows = [dgain[:, b * w : (b + 1) * w] for b in range(model // w)]
    place_rows(dst, at + 32, jnp.concatenate(rows + [empty(16 - len(rows))], axis=0))
    assert at + 48 == PACK


class Smalls:
    def __init__(self, line, square, pack, near, away, own, full, wide, sems):
        send, recv, keep, gsend, grecv, self.xsend, self.xrecv = sems
        self.square, self.full, self.wide = square, full, wide
        self.layers = range(pack.shape[0])
        self.sum = Scatter(line, pack, lambda j: own.at[j], near, away, send, recv)
        self.spread = Gather(line, lambda j: own.at[j], full, keep, gsend, grecv)

    def swap(self, k):
        sq = self.square
        slot = (sq.me, sq.me, lax.rem(sq.me + 2, 4))[k]
        who = (sq.across, sq.mate, sq.mate)[k]
        return remote(self.wide.at[slot], self.wide.at[slot], self.xsend.at[k], self.xrecv.at[k], who)

    def start(self):
        for j in self.layers:
            self.sum.start(j)

    def fold(self):
        for j in self.layers:
            for m in range(self.sum.line.n):
                self.sum.fold(j, m)

    def turn(self):
        for j in self.layers:
            self.sum.finish(j)
            self.spread.start(j)

    def relay(self, k):
        for j in self.layers:
            self.spread.relay(j, k)

    def cross(self):
        for j in self.layers:
            self.spread.arrive(j)
            flat = self.full[j].reshape(-1, self.full.shape[3])
            self.wide[self.square.me, j] = flat[: self.wide.shape[2]]
        self.swap(0).start()
        self.swap(1).start()

    def cross_on(self):
        self.swap(0).wait_recv()
        self.swap(2).start()

    def end(self):
        self.swap(1).wait_recv()
        self.swap(2).wait_recv()
        for k in range(3):
            self.swap(k).wait_send()
        for j in self.layers:
            self.sum.drain(j)
            self.spread.drain(j)


def smalls_scratch(size, w, layers):
    r, n = pack_rows(size), size // 2
    buffers = [
        pltpu.VMEM((layers, size, r, w), BF16),
        pltpu.VMEM((layers, n, r, w), BF16),
        pltpu.VMEM((layers, n, r, w), BF16),
        pltpu.VMEM((layers, r, w), BF16),
        pltpu.VMEM((layers, size, r, w), BF16),
        pltpu.VMEM((4, layers, SPAN, w), BF16),
    ]
    sems = [
        pltpu.SemaphoreType.DMA((2, layers, n)),
        pltpu.SemaphoreType.DMA((2, layers, n)),
        pltpu.SemaphoreType.DMA((layers,)),
        pltpu.SemaphoreType.DMA((layers, 3, size)),
        pltpu.SemaphoreType.DMA((layers, size)),
        pltpu.SemaphoreType.DMA((3,)),
        pltpu.SemaphoreType.DMA((3,)),
    ]
    return buffers + sems


def forward_body(*refs, size, heads, per, steps, layer):
    refs = list(refs)

    def take(n):
        got = refs[:n]
        del refs[:n]
        return got

    mid = layer > 0
    (res_hbm,) = take(1)
    if mid:
        scaled_hbm, wout_hbm, sq_ref = take(3)
    state_hbm, step_hbm, in_hbm, out_hbm, gain_ref = take(5)
    params = take(6)
    if mid:
        new_hbm, sums_ref = take(2)
    normed_hbm, rnorm_ref, small_hbm, inner_hbm, gate_hbm, wt_hbm, full_hbm, ssd_ref, scaled_ref, sqs_ref, st_ref = take(11)
    if mid:
        scaled_in, wout, part, got, far, other, rows_got, facs, fresh, sends, recvs, rsend, rrecv = take(13)
    res, wstate, wt, slabs, normed, turned, small, inner, gate, ext, exts, state = take(12)
    cp_ref, sp_ref, hp_ref, ind_ref, keep, gsend, grecv, load, sems = take(9)
    assert not refs

    n = CHUNK
    tokens_n, model = res.shape
    width = inner.shape[1]
    top = 2 * width + 2 * STATE
    i = pl.program_id(0)
    line = Line(size)
    square = Square()
    job = Gather(line, lambda j: out_hbm.at[layer] if j == 2 else in_hbm.at[layer, 1 - j], slabs, keep, gsend, grecv)
    outgoing = [(turned, normed_hbm), (small, small_hbm), (inner, inner_hbm), (gate, gate_hbm)]
    outgoing += [(wt, wt_hbm), (slabs.at[2], full_hbm)]
    if mid:
        outgoing.append((fresh, new_hbm))

    def flush(k):
        return pltpu.make_async_copy(*outgoing[k], sems.at[k])


    @pl.when(i == 0)
    def _():
        pairs = [(res_hbm, res), (state_hbm.at[layer], wstate), (step_hbm.at[layer], wt.at[pl.ds(top, LANES), :])]
        if mid:
            pairs = [(scaled_hbm, scaled_in), (wout_hbm, wout)] + pairs
        loads = [pltpu.make_async_copy(src, dst, load.at[k]) for k, (src, dst) in enumerate(pairs)]
        for copy in loads:
            copy.start()
        line.greet(pltpu.get_barrier_semaphore(), square.others() if mid else ())
        job.start(0)
        put_params(cp_ref, sp_ref, hp_ref, ind_ref, layer, params)
        ticks = [functools.partial(job.relay, 0, k) for k in range(1, line.n)]
        ticks.append(functools.partial(job.start, 1))
        span = model // LANES

        def project(j, dst):
            weight = slabs[j].reshape(model, width)

            def tile(t, _):
                rows = pl.ds(pl.multiple_of(t * TILE, TILE), TILE)
                dst[rows, :] = mm(normed[rows, :], weight)
                return 0

            lax.fori_loop(0, tokens_n // TILE, tile, 0)

        def turn_inner(b, _):
            wt[:width, pl.ds(pl.multiple_of(b * LANES, LANES), LANES)] = block_of(slabs.at[0], b, slabs.shape[2]).T
            return 0

        def settle():
            job.arrive(0)
            if not mid:
                project(0, inner)
                flush(2).start()
            lax.fori_loop(0, span, turn_inner, 0)

        ticks.append(functools.partial(job.relay, 1, 1))
        ticks.append(settle)
        ticks += [functools.partial(job.relay, 1, k) for k in range(2, line.n)]
        ticks.append(functools.partial(job.start, 2))

        if mid:
            chunks = model // SLICE
            half = tokens_n // 2
            sums = Total(square, part, got, far, other, sends, recvs)
            copies = [
                remote(sq_ref, rows_got.at[square.me], rsend.at[k], rrecv.at[k], who)
                for k, who in enumerate(square.others())
            ]
            for copy in copies:
                copy.start()
            loads[0].wait()
            loads[1].wait()
            for c in range(chunks):
                value = mm(scaled_in[...], wout[c * SLICE : (c + 1) * SLICE, :], NT).astype(BF16)
                part[2 * c] = value[:half]
                part[2 * c + 1] = value[half:]
                sums.step(0, c)
                if c:
                    sums.step(1, c - 1)
            sums.step(1, chunks - 1)
            rows_got[square.me] = sq_ref[...]
            for copy in copies:
                copy.wait()
            total = (rows_got[0] + rows_got[1]) + (rows_got[2] + rows_got[3])
            sums_ref[...] = total
            factor = lax.rsqrt(total / INNER + EPS)
            for t in range(tokens_n // LANES):
                facs[t * LANES : (t + 1) * LANES, :] = jnp.broadcast_to(factor[t], (LANES, LANES)).T
            loads[2].wait()

            def use(c):
                for h in range(2):
                    where = slice(h * half, (h + 1) * half)
                    for s in range(SLICE // LANES):
                        lanes = slice(c * SLICE + s * LANES, c * SLICE + (s + 1) * LANES)
                        value = part[2 * c + h, :, s * LANES : (s + 1) * LANES].astype(F32)
                        fresh[where, lanes] = res[where, lanes].astype(F32) + facs[where, :] * value

            spread = max(1, -(-len(ticks) // chunks))
            for c in range(chunks):
                for tick in ticks[:spread]:
                    tick()
                ticks = ticks[spread:]
                sums.step(2, c)
                if c:
                    sums.step(3, c - 1)
                    use(c - 1)
            sums.step(3, chunks - 1)
            use(chunks - 1)
            flush(6).start()
        else:
            loads[0].wait()
        loads[-2].wait()
        loads[-1].wait()
        for b in range(2 * STATE // LANES):
            rows = slice(2 * width + b * LANES, 2 * width + (b + 1) * LANES)
            wt[rows, :] = wstate[:, b * LANES : (b + 1) * LANES].T

        def norm(t, _):
            rows = pl.ds(pl.multiple_of(t * TILE, TILE), TILE)
            value = (fresh if mid else res)[rows, :].astype(F32)
            scale = lax.rsqrt(jnp.sum(value * value, axis=1, keepdims=True) / model + EPS)
            low = (value * scale * gain_ref[layer : layer + 1, :]).astype(BF16)
            rnorm_ref[rows, :] = scale
            normed[rows, :] = low
            turned[:, rows] = low.T
            small[rows, : 2 * STATE] = mm(low, wstate[...])
            small[rows, 2 * STATE :] = mm(low, wt[top:, :], NT)
            return 0

        lax.fori_loop(0, tokens_n // TILE, norm, 0)
        flush(0).start()
        flush(1).start()
        for tick in ticks:
            tick()

        if mid:
            project(0, inner)
            flush(2).start()
        job.arrive(1)
        project(1, gate)
        flush(3).start()

    for k in range(1, line.n):
        @pl.when(i == 1 + (k - 1) * steps // line.n)
        def _(k=k):
            job.relay(2, k)

    @pl.when(i > 0)
    def _():
        at = i - 1
        where = pl.ds(pl.multiple_of(at * n, n), n)

        @pl.when(lax.rem(at, per) == 0)
        def _():
            ext[0:8, :] = jnp.zeros((8, width), F32)
            exts[0:8, :] = jnp.zeros((8, 2 * STATE), F32)
            state[...] = jnp.zeros_like(state)

        rows, cols = iotas(n)
        ind = ind_ref[...]
        ext[8 : 8 + n, :] = inner[where, :]
        pre = conv_pre(ext, cp_ref, n)
        x = pre * sigmoid(pre)
        ext[0:8, :] = ext[n : n + 8, :]
        mini = small[where, :]
        exts[8 : 8 + n, :] = mini[:, : 2 * STATE]
        pres = conv_pre(exts, sp_ref, n)
        bc = (pres * sigmoid(pres)).astype(BF16)
        exts[0:8, :] = exts[n : n + 8, :]
        key, query = bc[:, :STATE], bc[:, STATE:]

        _, step, rate, cs, wide_step, wide_cs, wide_tail = scan_prep(mini, hp_ref, ind, n)
        cs2 = cs * LOG2E
        cs2t = cs2.T
        xs = x * wide_step
        lane = lax.broadcasted_iota(jnp.int32, (1, width), 1)
        half = jnp.where(lax.rem(lane, 2 * HEAD) < HEAD, 1.0, 0.0).astype(BF16)
        xsb = xs.astype(BF16)
        xs0 = xsb * half
        xs1 = xsb - xs0
        before = state[...]
        low = before.astype(BF16)
        st_ref[0] = low
        carried = mm(query, low) * wide_cs
        xw = (xs * wide_tail).astype(BF16)
        state[...] = before * wide_cs[n - 1 : n, :] + mm(key, xw, TN)
        scores = jnp.where(rows >= cols, mm(query, key, NT), 0.0)
        for pair in range(heads // 2):
            lanes = slice(pair * 2 * HEAD, (pair + 1) * 2 * HEAD)
            mats = []
            for h in (2 * pair, 2 * pair + 1):
                dec = jnp.exp2(jnp.minimum(cs2[:, h : h + 1] - cs2t[h : h + 1, :], 0.0))
                mats.append((scores * dec).astype(BF16))
            local = mm(
                jnp.concatenate(mats, axis=1),
                jnp.concatenate([xs0[:, lanes], xs1[:, lanes]], axis=0),
            )
            ssd_ref[:, lanes] = local + carried[:, lanes] + cp_ref[6:7, lanes] * x[:, lanes]
        gates = gate[where, :]
        gated = ssd_ref[...] * (gates * sigmoid(gates))
        sqs_ref[0] = rowsum(gated * gated)
        scaled_ref[...] = (gated * cp_ref[5:6, :]).astype(BF16)

        span = model // LANES
        share = -(-span // steps)
        for k in range(share):
            b = at * share + k

            @pl.when(b < span)
            def _(b=b):
                piece = block_of(slabs.at[1], b, slabs.shape[2]).T
                wt[width : 2 * width, pl.ds(pl.multiple_of(b * LANES, LANES), LANES)] = piece

    @pl.when(i == steps)
    def _():
        flush(4).start()
        job.arrive(2)
        flush(5).start()
        for j in range(3):
            job.drain(j)
        for k in range(len(outgoing)):
            flush(k).wait()


def forward(res, stateproj, steps_w, inproj, outt, gain, params, heads, size, layer, out=None):
    tokens_n, model = res.shape
    _, _, rows, width = inproj.shape
    top = 2 * width + 2 * STATE + LANES
    steps = tokens_n // CHUNK
    mid = out is not None
    hbm = pl.BlockSpec(memory_space=pl.ANY)
    chunks = model // SLICE

    def whole(a):
        return pl.BlockSpec(a.shape, lambda i: (0,) * len(a.shape))

    def row(w):
        return pl.BlockSpec((CHUNK, w), lambda i: (jnp.maximum(i - 1, 0), 0))

    args, in_specs, out_specs, out_shape, scratch = [res], [hbm], [], [], []
    if mid:
        args += list(out)
        in_specs += [hbm, hbm, whole(out[2])]
        out_specs += [hbm, whole(out[2])]
        out_shape += [jax.ShapeDtypeStruct(res.shape, F32), jax.ShapeDtypeStruct(out[2].shape, F32)]
        chunk = pltpu.VMEM((chunks, tokens_n // 2, SLICE), BF16)
        scratch += [
            pltpu.VMEM(out[0].shape, BF16),
            pltpu.VMEM(out[1].shape, BF16),
            pltpu.VMEM((2 * chunks, tokens_n // 2, SLICE), BF16),
            chunk, chunk, chunk,
            pltpu.VMEM((4,) + out[2].shape, F32),
            pltpu.VMEM((tokens_n, LANES), F32),
            pltpu.VMEM(res.shape, F32),
            pltpu.SemaphoreType.DMA((3, chunks)),
            pltpu.SemaphoreType.DMA((3, chunks)),
            pltpu.SemaphoreType.DMA((3,)),
            pltpu.SemaphoreType.DMA((3,)),
        ]
    args += [stateproj, steps_w, inproj, outt, gain, *params]
    in_specs += [hbm, hbm, hbm, hbm, whole(gain)] + [whole(v) for v in params]
    out_specs += [
        hbm, pl.BlockSpec((tokens_n, 1), lambda i: (0, 0)), hbm, hbm, hbm, hbm, hbm,
        row(width), row(width),
        pl.BlockSpec((1, 1, CHUNK), lambda i: (jnp.maximum(i - 1, 0), 0, 0)),
        pl.BlockSpec((1, STATE, width), lambda i: (jnp.maximum(i - 1, 0), 0, 0)),
    ]
    out_shape += [
        jax.ShapeDtypeStruct((model, tokens_n), BF16),
        jax.ShapeDtypeStruct((tokens_n, 1), F32),
        jax.ShapeDtypeStruct((tokens_n, 2 * STATE + LANES), F32),
        jax.ShapeDtypeStruct((tokens_n, width), F32),
        jax.ShapeDtypeStruct((tokens_n, width), F32),
        jax.ShapeDtypeStruct((top, model), BF16),
        jax.ShapeDtypeStruct((size, rows, width), BF16),
        jax.ShapeDtypeStruct((tokens_n, width), F32),
        jax.ShapeDtypeStruct((tokens_n, width), BF16),
        jax.ShapeDtypeStruct((steps, 1, CHUNK), F32),
        jax.ShapeDtypeStruct((steps, STATE, width), BF16),
    ]
    scratch += [
        pltpu.VMEM(res.shape, res.dtype),
        pltpu.VMEM((model, 2 * STATE), BF16),
        pltpu.VMEM((top, model), BF16),
        pltpu.VMEM((3, size, rows, width), BF16),
        pltpu.VMEM((tokens_n, model), BF16),
        pltpu.VMEM((model, tokens_n), BF16),
        pltpu.VMEM((tokens_n, 2 * STATE + LANES), F32),
        pltpu.VMEM((tokens_n, width), F32),
        pltpu.VMEM((tokens_n, width), F32),
        pltpu.VMEM((CHUNK + 8, width), F32),
        pltpu.VMEM((CHUNK + 8, 2 * STATE), F32),
        pltpu.VMEM((STATE, width), F32),
        pltpu.VMEM((8, width), F32),
        pltpu.VMEM((8, 2 * STATE), F32),
        pltpu.VMEM((8, LANES), F32),
        pltpu.VMEM((LANES, width), BF16),
        pltpu.SemaphoreType.DMA((3,)),
        pltpu.SemaphoreType.DMA((3, 3, size)),
        pltpu.SemaphoreType.DMA((3, size)),
        pltpu.SemaphoreType.DMA((5,)),
        pltpu.SemaphoreType.DMA((7,)),
    ]
    return pl.pallas_call(
        functools.partial(forward_body, size=size, heads=heads, per=LEN // CHUNK, steps=steps, layer=layer),
        grid=(steps + 1,),
        in_specs=in_specs,
        out_specs=out_specs,
        out_shape=out_shape,
        scratch_shapes=scratch,
        compiler_params=pltpu.CompilerParams(
            collective_id=min(layer, 1), has_side_effects=True, vmem_limit_bytes=VMEM_LIMIT
        ),
        name="forward",
    )(*args)


def back_body(*refs, heads, per, size, steps, layer, last):
    refs = list(refs)

    def take(n):
        got = refs[:n]
        del refs[:n]
        return got

    up_ref, sq_ref, gate_ref, ssd_ref, inner_ref, iprev_ref, small_ref, sprev_ref, st_ref, res_ref, rn_ref = take(11)
    gain_ref = take(1)[0]
    params = take(6)
    wout_hbm, scaled_hbm, wt_hbm, normed_hbm = take(4)
    if not last:
        next_normed, next_steps, next_sdel, next_inner, next_dcp, next_dsp, next_dhp, next_dgain = take(8)
    new_ref, grad_hbm = take(2)
    if last:
        held_hbm, sdsum_ref, steplow_ref, dcp_ref, dsp_ref, dhp_ref, dgain_ref, mixed_ref = take(8)
    else:
        full_hbm, wide_hbm = take(2)
    ext, exts, cde, cdes, dstate, rq, cp_ref, sp_ref, hp_ref, ind_ref = take(10)
    wout, scaled, wt, turned, dy, glow, ilow, frow, srow, sgot = take(10)
    part, near, away, tpart, got, far, other = take(7)
    load, rsend, rrecv, ssend, srecv, sends, recvs, gsem = take(8)
    if last:
        held, fgot, opart, ogot, ofar, oother, fsend, frecv, osends, orecvs = take(10)
    else:
        dcp_ref, dsp_ref, dhp_ref, dgain_ref = take(4)
        sd_all = scaled.at[:, pl.ds(0, 2 * STATE)]
        step_all = scaled.at[:, pl.ds(2 * STATE, LANES)]
        buffers = take(6)
        sems = take(7)
    assert not refs

    n = CHUNK
    model = up_ref.shape[1]
    i = pl.program_id(0)
    begin_gate = steps
    begin_scan = begin_gate + steps
    begin_norm = begin_scan + steps
    end = begin_norm + steps - 1
    line = Line(size)
    square = Square()
    rows_own = part.shape[2]
    count = part.shape[0]
    job = Scatter(line, part, lambda j: dy.at[pl.ds(j * rows_own, rows_own), :], near, away, ssend, srecv)
    sums = Total(square, tpart, got, far, other, sends, recvs)
    if last:
        outs = Total(square, opart, ogot, ofar, oother, osends, orecvs)
        half = steps * n // 2
        slices = model // SLICE
    else:
        minis = Smalls(line, square, *buffers, sems)
    moves = [(wout_hbm, wout), (scaled_hbm, scaled), (wt_hbm, wt), (normed_hbm, turned)]
    if last:
        moves.append((held, held_hbm))
    else:
        tokens_n = steps * n
        spots = (wt.at[pl.ds(0, model), pl.ds(0, tokens_n)],)
        spots += tuple(
            wt.at[pl.ds(0, tokens_n), pl.ds(tokens_n + at, w)] for at, w in ((0, LANES), (LANES, 2 * STATE))
        )
        moves += [(next_normed, spots[0]), (next_steps, spots[1]), (next_sdel, spots[2]), (next_inner, part.at[3])]

    def move(k):
        return pltpu.make_async_copy(*moves[k], load.at[k])

    places = line.n

    def spaced(begin, stop, m):
        return begin + m * (stop - begin) // places

    middle = begin_scan + steps // 2
    if last:
        folds = [(spaced(begin_scan, middle, m), 0, m) for m in range(places)]
        folds += [(spaced(middle, begin_norm, m) + 1, 1, m) for m in range(places)]
    else:
        folds = [(spaced(begin_gate - 1, begin_scan + 3, m), 3, m) for m in range(places)]
        folds += [(spaced(begin_scan + 2, middle + 3, m), 0, m) for m in range(places)]
        folds += [(spaced(begin_norm - 1, end - 1, m), 1, m) for m in range(places)]

    def column(row):
        return jnp.broadcast_to(row, (n, n)).T[:, 0:1]

    @pl.when(i == 0)
    def _():
        for k in range(3):
            move(k).start()
        if not last:
            move(7).start()
        put_params(cp_ref, sp_ref, hp_ref, ind_ref, layer, params)
        rq[...] = jnp.zeros_like(rq)
        line.greet_all(pltpu.get_barrier_semaphore(), square.others())
        if last:
            rows = [
                remote(sq_ref, fgot.at[square.me], fsend.at[k], frecv.at[k], who)
                for k, who in enumerate(square.others())
            ]
            for copy in rows:
                copy.start()
            fgot[square.me] = sq_ref[...]
            move(0).wait()
            move(1).wait()
            for c in range(slices):
                value = mm(scaled[...], wout[c * SLICE : (c + 1) * SLICE, :], NT).astype(BF16)
                opart[2 * c] = value[:half]
                opart[2 * c + 1] = value[half:]
                outs.step(0, c)
            outs.step(1, 0)
            for copy in rows:
                copy.wait()
            total = (fgot[0] + fgot[1]) + (fgot[2] + fgot[3])
        else:
            move(7).wait()
            job.start(3)
            total = sq_ref[...]
            move(0).wait()
            move(1).wait()
        dcp_ref[...] = jnp.zeros_like(dcp_ref)
        dsp_ref[...] = jnp.zeros_like(dsp_ref)
        dhp_ref[...] = jnp.zeros_like(dhp_ref)
        dgain_ref[...] = jnp.zeros_like(dgain_ref)
        frow[...] = lax.rsqrt(total / INNER + EPS)

    ind = ind_ref[...]
    for at, j, m in folds:
        @pl.when(i == at)
        def _(j=j, m=m):
            job.fold(j, m)

    @pl.when(i < begin_gate)
    def _():
        rows = pl.ds(pl.multiple_of(i * n, n), n)
        low = (column(frow[i]) * up_ref[...].astype(F32)).astype(BF16)
        turned[:, rows] = low.T
        sd = mm(low, wout[...])
        dy[rows, :] = sd
        piece = scaled[rows, :]
        srow[i] = rowsum(piece.astype(F32) * sd)

    @pl.when(i == begin_gate - 1)
    def _():
        copies = [
            remote(srow, sgot.at[square.me], rsend.at[k], rrecv.at[k], who) for k, who in enumerate(square.others())
        ]
        for copy in copies:
            copy.start()
        job.emit(0, turned, scaled)
        move(3).start()
        sgot[square.me] = srow[...]
        for copy in copies:
            copy.wait()
        srow[...] = (sgot[0] + sgot[1]) + (sgot[2] + sgot[3])

    if last:
        @pl.when(i == steps // 2)
        def _():
            outs.step(1, 1)

        @pl.when((i >= begin_gate) & (i < begin_gate + slices - 2))
        def _():
            outs.step(1, i - begin_gate + 2)

    @pl.when((i >= begin_gate) & (i < begin_scan))
    def _():
        c = i - begin_gate
        rows = pl.ds(pl.multiple_of(c * n, n), n)
        coef = column(frow[c] * frow[c] * srow[c]) / INNER
        gate = gate_ref[...]
        gsig = sigmoid(gate)
        gact = gate * gsig
        ssd = ssd_ref[...]
        sd = dy[rows, :]
        gated = ssd * gact
        gd = cp_ref[5:6, :] * sd - coef * gated
        dcp_ref[5:6, :] += colsum(gated * sd)
        dy[rows, :] = gd * gact
        glow[rows, :] = (gd * ssd * (gsig + gact * (1.0 - gsig))).astype(BF16)

    @pl.when(i == begin_scan - 1)
    def _():
        move(3).wait()
        job.emit(1, turned, glow)
        move(2).wait()

    @pl.when((i >= begin_scan) & (i < begin_norm))
    def _():
        q = i - begin_scan
        chunk = steps - 1 - q
        where = pl.ds(pl.multiple_of(chunk * n, n), n)

        @pl.when(lax.rem(chunk, per) == per - 1)
        def _():
            cde[n : n + 8, :] = jnp.zeros((8, cde.shape[1]), F32)
            cdes[n : n + 8, :] = jnp.zeros((8, cdes.shape[1]), F32)
            dstate[...] = jnp.zeros_like(dstate)

        keep = jnp.where(lax.rem(chunk, per) == 0, 0.0, 1.0).astype(F32)
        rows, cols = iotas(n)
        ext[0:8, :] = iprev_ref[...] * keep
        ext[8 : 8 + n, :] = inner_ref[...]
        exts[0:8, :] = sprev_ref[:, : 2 * STATE] * keep
        exts[8 : 8 + n, :] = small_ref[:, : 2 * STATE]
        pre = conv_pre(ext, cp_ref, n)
        sig = sigmoid(pre)
        x = pre * sig
        slope = sig + x * (1.0 - sig)
        pres = conv_pre(exts, sp_ref, n)
        sigs = sigmoid(pres)
        acts = pres * sigs
        slopes = sigs + acts * (1.0 - sigs)
        bc = acts.astype(BF16)
        key, query = bc[:, :STATE], bc[:, STATE:]
        dyc = dy[where, :]

        raw, step, rate, cs, wide_step, wide_cs, wide_tail = scan_prep(small_ref, hp_ref, ind, n)
        cs2 = cs * LOG2E
        cs2t = cs2.T
        xs = x * wide_step
        xsb = xs.astype(BF16)
        dyb = dyc.astype(BF16)
        lane = lax.broadcasted_iota(jnp.int32, (1, xs.shape[1]), 1)
        half = jnp.where(lax.rem(lane, 2 * HEAD) < HEAD, 1.0, 0.0).astype(BF16)
        dy0 = dyb * half
        dy1 = dyb - dy0
        low = st_ref[0]
        dst = dstate[...]
        dlow = dst.astype(BF16)
        dye = dyc * wide_cs
        dyeb = dye.astype(BF16)
        up = headsum(dye * mm(query, low), ind)
        dxs_state = wide_tail * mm(key, dlow)
        down = headsum(xs * dxs_state, ind)
        qdel = mm(dyeb, low, NT)
        kdel = mm((xs * wide_tail).astype(BF16), dlow, NT)
        through = headsum(jnp.broadcast_to(colsum(low.astype(F32) * dst), (8, dst.shape[1])), ind)[0:1, :]
        through = through * jnp.exp(cs[n - 1 : n, :])
        dstate[...] = dst * wide_cs[n - 1 : n, :] + mm(query, dyeb, TN)

        scores = jnp.where(rows <= cols, mm(key, query, NT), 0.0)
        dscores = jnp.zeros((n, n), F32)
        colq = jnp.zeros((n, LANES), F32)
        lane = lax.broadcasted_iota(jnp.int32, (n, LANES), 1)
        dxs = []
        for pair in range(heads // 2):
            lanes = slice(pair * 2 * HEAD, (pair + 1) * 2 * HEAD)
            stacked = jnp.concatenate([dy0[:, lanes], dy1[:, lanes]], axis=0)
            both = mm(xsb[:, lanes], stacked, NT)
            mats = []
            for which, h in enumerate((2 * pair, 2 * pair + 1)):
                dec = jnp.exp2(jnp.minimum(cs2t[h : h + 1, :] - cs2[:, h : h + 1], 0.0))
                mats.append((scores * dec).astype(BF16))
                term = dec * both[:, which * n : (which + 1) * n]
                dscores = dscores + term
                quad = scores * term
                rq[h : h + 1, :] = colsum(quad)
                colq = jnp.where(lane == h, jnp.sum(quad, axis=1, keepdims=True), colq)
            dxs.append(mm(jnp.concatenate(mats, axis=1), stacked))
        dxs = jnp.concatenate(dxs, axis=1) + dxs_state
        dscores = jnp.where(rows <= cols, dscores, 0.0).astype(BF16)
        kdel = kdel + mm(dscores, query)
        qdel = qdel + mm(dscores, key, TN)

        upper = jnp.where(rows <= cols, 1.0, 0.0).astype(F32)
        strict = jnp.where(rows > cols, 1.0, 0.0).astype(F32)
        da = mm(upper, rq[...].T - colq + up, precision=HIGH) + mm(strict, down, precision=HIGH) + through
        grown = headsum(x * dxs, ind) + rate * da
        step_pre = grown * sigmoid(raw)
        steplow = step_pre.astype(BF16)
        if last:
            steplow_ref[...] = steplow
        else:
            step_all[where, :] = steplow
        dhp_ref[0:1, :] += colsum(step_pre)
        dhp_ref[1:2, :] += rate * colsum(step * da)
        dcp_ref[6:7, :] += colsum(dyc * x)

        cd = (dxs * wide_step + cp_ref[6:7, :] * dyc) * slope
        cde[0:n, :] = cd
        center = ext[8 : 8 + n, :]
        total = cp_ref[3:4, :] * cd
        dcp_ref[3:4, :] += colsum(cd * center)
        for tap in range(3):
            shifted = cde[3 - tap : 3 - tap + n, :]
            total = total + cp_ref[tap : tap + 1, :] * shifted
            dcp_ref[tap : tap + 1, :] += colsum(shifted * center)
        inner_low = total.astype(BF16)
        ilow[where, :] = inner_low
        dcp_ref[4:5, :] += colsum(cd)
        cde[n : n + 8, :] = cde[0:8, :]

        cds = jnp.concatenate([kdel, qdel], axis=1) * slopes
        cdes[0:n, :] = cds
        center = exts[8 : 8 + n, :]
        total = sp_ref[3:4, :] * cds
        dsp_ref[3:4, :] += colsum(cds * center)
        for tap in range(3):
            shifted = cdes[3 - tap : 3 - tap + n, :]
            total = total + sp_ref[tap : tap + 1, :] * shifted
            dsp_ref[tap : tap + 1, :] += colsum(shifted * center)
        sdel = total.astype(BF16)
        dsp_ref[4:5, :] += colsum(cds)
        cdes[n : n + 8, :] = cdes[0:8, :]

        lows = jnp.concatenate([inner_low, glow[where, :], sdel, steplow], axis=1)
        value = mm(lows, wt[...]).astype(BF16)
        tpart[2 * q, :, :model] = value[: n // 2]
        tpart[2 * q + 1, :, :model] = value[n // 2 :]
        tpart[2 * q, :, model:] = sdel[: n // 2]
        tpart[2 * q + 1, :, model:] = sdel[n // 2 :]
        sums.step(0, q)

    @pl.when((i > begin_scan) & (i <= begin_norm))
    def _():
        sums.step(1, i - begin_scan - 1)

    @pl.when((i >= begin_scan + 5) & (i < begin_norm + 5))
    def _():
        sums.step(2, i - begin_scan - 5)

    @pl.when((i >= begin_scan + 6) & (i < begin_norm + 6))
    def _():
        sums.step(3, i - begin_scan - 6)

    if last:
        @pl.when((i > begin_scan) & (i <= begin_scan + slices))
        def _():
            outs.step(2, i - begin_scan - 1)

        @pl.when((i > begin_scan + 1) & (i <= begin_scan + slices + 1))
        def _():
            outs.step(3, i - begin_scan - 2)

    @pl.when(i == begin_norm - 1)
    def _():
        dhp_ref[2:3, :] = headsum(jnp.broadcast_to(dcp_ref[6:7, :], (8, dcp_ref.shape[1])), ind)[0:1, :]
        if last:
            job.product(held, turned, ilow)
            move(4).start()
        else:
            job.emit(2, turned, ilow, places // 2)
            for k in (4, 5, 6):
                move(k).start()

    if not last:
        @pl.when(i == begin_norm + 1)
        def _():
            for k in (4, 5, 6):
                move(k).wait()
            put_pack(
                buffers[0].at[1], square.me, *spots, next_dcp[...], next_dsp[...], next_dhp[...], next_dgain[...]
            )
            minis.sum.start(1)

    @pl.when(i >= begin_norm)
    def _():
        r = i - begin_norm
        chunk = steps - 1 - r
        if last:
            fac = column(frow[chunk])
            side = chunk // (steps // 2)
            base = (chunk - side * (steps // 2)) * n
        for h in range(2):
            rows = slice(h * (n // 2), (h + 1) * (n // 2))
            back = tpart[2 * r + h, :, :model].astype(F32)
            sdel = tpart[2 * r + h, :, model:]
            if last:
                sdsum_ref[rows, :] = sdel
            else:
                sd_all[pl.ds(pl.multiple_of(chunk * n + h * (n // 2), n // 2), n // 2), :] = sdel
            res = res_ref[rows, :].astype(F32)
            rn = rn_ref[rows, :]
            dgain_ref[...] += colsum(back * res * rn)
            gained = back * gain_ref[layer : layer + 1, :]
            mean = jnp.sum(gained * res, axis=1, keepdims=True) / model
            new_ref[rows, :] = up_ref[rows, :].astype(F32) + rn * gained - (rn * rn * rn * mean) * res
            if last:
                where = pl.ds(pl.multiple_of(base + h * (n // 2), n // 2), n // 2)
                for c in range(slices):
                    span = slice(c * SLICE, (c + 1) * SLICE)
                    summed = opart[2 * c + side, where, :].astype(F32)
                    mixed_ref[rows, span] = (res[:, span] + fac[rows, :] * summed).astype(BF16)

    @pl.when(i == end)
    def _():
        def finish(j):
            job.finish(j)
            pltpu.make_async_copy(dy.at[pl.ds(j * rows_own, rows_own), :], grad_hbm.at[j], gsem.at[j]).start()

        if not last:
            put_pack(
                buffers[0].at[0], square.me, turned, step_all, sd_all, dcp_ref[...], dsp_ref[...], dhp_ref[...], dgain_ref[...]
            )
            minis.sum.start(0)
            for m in range(places // 2, places - 1):
                job.lead(2, m)
            for m in range(places // 2):
                job.fold(2, m)
            finish(3)
        finish(0)
        finish(1)
        if not last:
            minis.fold()
            minis.turn()
            for k in range(1, line.n):
                minis.relay(k)
            job.lead(2, places - 1)
            for m in range(places // 2, places):
                job.fold(2, m)
            minis.cross()
            finish(2)
            minis.cross_on()
            minis.end()
            tails = [
                pltpu.make_async_copy(src, dst, load.at[k])
                for k, (src, dst) in enumerate(((minis.full, full_hbm), (minis.wide, wide_hbm)))
            ]
            for copy in tails:
                copy.start()
        for j in range(count):
            job.drain(j)
            pltpu.make_async_copy(dy.at[pl.ds(j * rows_own, rows_own), :], grad_hbm.at[j], gsem.at[j]).wait()
        if last:
            move(4).wait()
        else:
            for copy in tails:
                copy.wait()


def back(up, sq, gate_pre, ssd, inner_raw, small, states, res, rnorm, gain, params,
         wout, scaled, wt, normed, heads, size, layer, after=None):
    tokens_n, width = inner_raw.shape
    model = up.shape[1]
    last = after is None
    steps = tokens_n // CHUNK
    begin_scan = 2 * steps
    begin_norm = begin_scan + steps
    rows = model // size
    n = size // 2
    hbm = pl.BlockSpec(memory_space=pl.ANY)
    top = steps - 1

    def norm_at(i):
        return jnp.where(i < begin_norm, top, top - (i - begin_norm))

    def scan_at(i):
        return jnp.clip(top - (i - begin_scan), 0, top)

    def first(w):
        return pl.BlockSpec((CHUNK, w), lambda i: (jnp.where(i < steps, i, norm_at(i)), 0))

    def second(w):
        return pl.BlockSpec((CHUNK, w), lambda i: (jnp.clip(i - steps, 0, top), 0))

    def scan(w):
        return pl.BlockSpec((CHUNK, w), lambda i: (scan_at(i), 0))

    def prev(w):
        return pl.BlockSpec((8, w), lambda i: (jnp.maximum(scan_at(i) * (CHUNK // 8) - 1, 0), 0))

    def norm(w):
        return pl.BlockSpec((CHUNK, w), lambda i: (norm_at(i), 0))

    def whole(a):
        return pl.BlockSpec(a.shape, lambda i: (0,) * len(a.shape))

    extra = model + 2 * STATE
    quarter = pltpu.VMEM((steps, CHUNK // 2, extra), BF16)
    count = 2 if last else 4
    pieces = pltpu.VMEM((count, n, rows, width), BF16)
    args = [up, sq, gate_pre, ssd, inner_raw, inner_raw, small, small, states, res, rnorm, gain, *params,
            wout, scaled, wt, normed]
    in_specs = [
        first(model), whole(sq), second(width), second(width),
        scan(width), prev(width), scan(small.shape[1]), prev(small.shape[1]),
        pl.BlockSpec((1, STATE, width), lambda i: (scan_at(i), 0, 0)),
        norm(model), norm(1), whole(gain),
    ] + [whole(a) for a in params] + [hbm] * 4
    out_specs = [norm(model), hbm]
    out_shape = [jax.ShapeDtypeStruct((tokens_n, model), F32), jax.ShapeDtypeStruct((count, rows, width), F32)]
    totals = [(8, width), (8, 2 * STATE), (8, LANES), (1, model)]
    scratch = [
        pltpu.VMEM((CHUNK + 8, width), F32),
        pltpu.VMEM((CHUNK + 8, 2 * STATE), F32),
        pltpu.VMEM((CHUNK + 8, width), F32),
        pltpu.VMEM((CHUNK + 8, 2 * STATE), F32),
        pltpu.VMEM((STATE, width), F32),
        pltpu.VMEM((LANES, CHUNK), F32),
        pltpu.VMEM((8, width), F32),
        pltpu.VMEM((8, 2 * STATE), F32),
        pltpu.VMEM((8, LANES), F32),
        pltpu.VMEM((LANES, width), BF16),
        pltpu.VMEM(wout.shape, BF16),
        pltpu.VMEM(scaled.shape, BF16),
        pltpu.VMEM(wt.shape, BF16),
        pltpu.VMEM(normed.shape, BF16),
        pltpu.VMEM((tokens_n, width), F32),
        pltpu.VMEM((tokens_n, width), BF16),
        pltpu.VMEM((tokens_n, width), BF16),
        pltpu.VMEM((steps, 1, CHUNK), F32),
        pltpu.VMEM((steps, 1, CHUNK), F32),
        pltpu.VMEM((4, steps, 1, CHUNK), F32),
        pltpu.VMEM((count, size, rows, width), BF16), pieces, pieces,
        pltpu.VMEM((2 * steps, CHUNK // 2, extra), BF16), quarter, quarter, quarter,
        pltpu.SemaphoreType.DMA((8,)),
        pltpu.SemaphoreType.DMA((3,)),
        pltpu.SemaphoreType.DMA((3,)),
        pltpu.SemaphoreType.DMA((2, count, n)),
        pltpu.SemaphoreType.DMA((2, count, n)),
        pltpu.SemaphoreType.DMA((3, steps)),
        pltpu.SemaphoreType.DMA((3, steps)),
        pltpu.SemaphoreType.DMA((count,)),
    ]
    if last:
        out_specs += [hbm, norm(2 * STATE), scan(LANES)]
        out_specs += [pl.BlockSpec(v, lambda i: (0, 0)) for v in totals] + [norm(model)]
        out_shape += [
            jax.ShapeDtypeStruct((size, rows, width), BF16),
            jax.ShapeDtypeStruct((tokens_n, 2 * STATE), BF16),
            jax.ShapeDtypeStruct((tokens_n, LANES), BF16),
        ]
        out_shape += [jax.ShapeDtypeStruct(v, F32) for v in totals]
        out_shape.append(jax.ShapeDtypeStruct((tokens_n, model), BF16))
        slices = model // SLICE
        chunk = pltpu.VMEM((slices, tokens_n // 2, SLICE), BF16)
        scratch += [
            pltpu.VMEM((size, rows, width), BF16),
            pltpu.VMEM((4, steps, 1, CHUNK), F32),
            pltpu.VMEM((2 * slices, tokens_n // 2, SLICE), BF16), chunk, chunk, chunk,
            pltpu.SemaphoreType.DMA((3,)),
            pltpu.SemaphoreType.DMA((3,)),
            pltpu.SemaphoreType.DMA((3, slices)),
            pltpu.SemaphoreType.DMA((3, slices)),
        ]
    else:
        w = 2 * STATE
        r = pack_rows(size)
        args += list(after)
        in_specs += [hbm] * 4 + [whole(v) for v in after[4:]]
        out_specs += [hbm, hbm]
        out_shape += [
            jax.ShapeDtypeStruct((2, size, r, w), BF16),
            jax.ShapeDtypeStruct((4, 2, SPAN, w), BF16),
        ]
        scratch += [pltpu.VMEM(v, F32) for v in totals]
        scratch += smalls_scratch(size, w, 2)
    return pl.pallas_call(
        functools.partial(
            back_body, heads=heads, per=LEN // CHUNK, size=size, steps=steps, layer=layer, last=last
        ),
        grid=(begin_norm + steps,),
        in_specs=in_specs,
        out_specs=out_specs,
        out_shape=out_shape,
        scratch_shapes=scratch,
        compiler_params=pltpu.CompilerParams(
            collective_id=2 if last else 3, has_side_effects=True, vmem_limit_bytes=VMEM_LIMIT
        ),
        name="back",
    )(*args)


def results_body(full_ref, wide_ref, first_hbm, second_hbm, mixed_hbm, up_hbm, *refs, layers, heads):
    pair_out, out_out, mixed_out, up_out = refs[11:15]
    first, second, mixed, up, load, store = refs[15:]
    refs = refs[:11]
    loads = [
        pltpu.make_async_copy(src, dst, load.at[k])
        for k, (src, dst) in enumerate(((up_hbm, up), (mixed_hbm, mixed), (first_hbm, first), (second_hbm, second)))
    ]
    for copy in loads:
        copy.start()
    step_ref, state_ref, conv_ref, bias_ref, convs_ref, biass_ref = refs[:6]
    stepbias_ref, decay_ref, skip_ref, norm_ref, gain_ref = refs[6:]
    model = state_ref.shape[1]
    quarter = model // 4
    w = state_ref.shape[2]
    width = conv_ref.shape[2]
    for layer in range(layers):
        for t in range(4):
            state_ref[layer, t * quarter : (t + 1) * quarter, :] = wide_ref[t, layer, :quarter, :].astype(F32)
        taps = [wide_ref[t, layer, quarter : quarter + 16, :].astype(F32) for t in range(4)]
        taps = (taps[0] + taps[1]) + (taps[2] + taps[3])
        convs_ref[layer] = taps[0:4]
        biass_ref[layer : layer + 1, :] = taps[4:5]
        flat = full_ref[layer].reshape(-1, w)[:PACK].astype(F32)
        at = quarter + 16
        for b in range(model // w):
            step_ref[layer, :, b * w : (b + 1) * w] = flat[at : at + 16]
            at += 16
        for b in range(width // w):
            lanes = slice(b * w, (b + 1) * w)
            rows = flat[at + 8 * b : at + 8 * b + 8]
            conv_ref[layer, :, lanes] = rows[0:4]
            bias_ref[layer : layer + 1, lanes] = rows[4:5]
            norm_ref[layer : layer + 1, lanes] = rows[5:6]
        at += 8 * (width // w)
        for k, ref in enumerate((stepbias_ref, decay_ref, skip_ref)):
            ref[layer : layer + 1, :] = flat[at + k : at + k + 1, :heads]
        at += 8
        for b in range(model // w):
            gain_ref[layer : layer + 1, b * w : (b + 1) * w] = flat[at + b : at + b + 1]
    for copy in loads:
        copy.wait()
    moves = [
        (up, up_out), (mixed, mixed_out), (first.at[pl.ds(1, 2)], pair_out.at[0]), (second.at[1], pair_out.at[1, 0]),
        (first.at[3], pair_out.at[1, 1]), (first.at[0], out_out.at[0]), (second.at[0], out_out.at[1]),
    ]
    stores = [pltpu.make_async_copy(src, dst, store.at[k]) for k, (src, dst) in enumerate(moves)]
    for copy in stores:
        copy.start()
    for copy in stores:
        copy.wait()


def write_results(full, wide, first, second, mixed, up, heads):
    layers, w = full.shape[0], full.shape[3]
    _, rows, width = first.shape
    model = up.shape[1]
    vm = pl.BlockSpec(memory_space=pltpu.VMEM)
    hbm = pl.BlockSpec(memory_space=pl.ANY)
    shapes = [
        (layers, 16, model), (layers, model, w), (layers, 4, width), (layers, width), (layers, 4, w), (layers, w),
        (layers, heads), (layers, heads), (layers, heads), (layers, width), (layers, model),
    ]
    return pl.pallas_call(
        functools.partial(results_body, layers=layers, heads=heads),
        in_specs=[vm, vm] + [hbm] * 4,
        out_specs=[vm] * len(shapes) + [hbm] * 4,
        out_shape=[jax.ShapeDtypeStruct(v, F32) for v in shapes] + [
            jax.ShapeDtypeStruct((layers, 2, rows, width), F32),
            jax.ShapeDtypeStruct((layers, rows, width), F32),
            jax.ShapeDtypeStruct(mixed.shape, mixed.dtype),
            jax.ShapeDtypeStruct(up.shape, up.dtype),
        ],
        scratch_shapes=[
            pltpu.VMEM(first.shape, F32),
            pltpu.VMEM(second.shape, F32),
            pltpu.VMEM(mixed.shape, mixed.dtype),
            pltpu.VMEM(up.shape, up.dtype),
            pltpu.SemaphoreType.DMA((4,)),
            pltpu.SemaphoreType.DMA((7,)),
        ],
        compiler_params=pltpu.CompilerParams(vmem_limit_bytes=VMEM_LIMIT),
        name="results",
    )(full, wide, first, second, mixed, up)


def shards(
    tokens, inproj, stepproj, stateproj, outproj, convinner, biasinner, convstate, biasstate,
    stepbias, decaylog, skipgain, normgain, inputgain, cotangent,
):
    layers = inproj.shape[0]
    width = inproj.shape[3]
    heads = stepproj.shape[2]
    model = tokens.shape[1]
    pad = LANES - heads
    size = lax.axis_size("dp")
    steps_w = jnp.pad(jnp.swapaxes(stepproj, 1, 2), ((0, 0), (0, pad), (0, 0)))
    head = jnp.pad(jnp.stack([stepbias, decaylog, skipgain], axis=1), ((0, 0), (0, 5), (0, pad)))
    outt = jnp.swapaxes(outproj, 1, 2)
    params = (convinner, biasinner, normgain, convstate, biasstate, head)

    residual = tokens
    kept = []
    out = None
    for at in range(layers):
        results = forward(residual, stateproj, steps_w, inproj, outt, inputgain, params, heads, size, at, out=out)
        if at:
            residual, kept[-1][-1] = results[:2]
            results = results[2:]
        normed, rnorm, small, inner_raw, gate_pre, wt, w_out, ssd, scaled, sq, states = results
        w_out = w_out.reshape(model, width)
        kept.append([residual, normed, rnorm, small, inner_raw, gate_pre, wt, w_out, ssd, scaled, states, sq])
        out = (scaled, w_out, sq)

    assert layers == 2
    before, normed, rnorm, small, inner_raw, gate_pre, wt, w_out, ssd, scaled, states, sq = kept[1]
    upstream, second, held, sdel, steplow, *totals, mixed = back(
        cotangent, sq, gate_pre, ssd, inner_raw, small, states, before, rnorm, inputgain, params,
        w_out, scaled, wt, normed, heads, size, 1,
    )
    after = (normed, steplow, sdel, held, *totals)
    before, normed, rnorm, small, inner_raw, gate_pre, wt, w_out, ssd, scaled, states, sq = kept[0]
    upstream, first, full, wide = back(
        upstream, sq, gate_pre, ssd, inner_raw, small, states, before, rnorm, inputgain, params,
        w_out, scaled, wt, normed, heads, size, 0, after=after,
    )
    (
        step_grad, state_grad, conv_grad, bias_grad, convs_grad, biass_grad,
        stepbias_grad, decay_grad, skip_grad, norm_grad, gain_grad, pair_grad, out_grad, mixed, upstream,
    ) = write_results(full, wide, first, second, mixed, upstream, heads)
    return (
        mixed,
        upstream,
        pair_grad,
        jnp.swapaxes(step_grad[:, :heads], 1, 2),
        state_grad,
        jnp.swapaxes(out_grad, 1, 2),
        conv_grad,
        bias_grad,
        convs_grad,
        biass_grad,
        stepbias_grad,
        decay_grad,
        skip_grad,
        norm_grad,
        gain_grad,
    )


def solution(mesh):
    in_specs = (
        P("dp", None),
        P(None, None, "dp", "tensor"),
        P(None, None, "tensor"),
        P(),
        P(None, "tensor", "dp"),
        P(None, None, "tensor"),
        P(None, "tensor"),
        P(),
        P(),
        P(None, "tensor"),
        P(None, "tensor"),
        P(None, "tensor"),
        P(None, "tensor"),
        P(),
        P("dp", None),
    )
    out_specs = (
        P("dp", None),
        P("dp", None),
        P(None, None, "dp", "tensor"),
        P(None, None, "tensor"),
        P(),
        P(None, "tensor", "dp"),
        P(None, None, "tensor"),
        P(None, "tensor"),
        P(),
        P(),
        P(None, "tensor"),
        P(None, "tensor"),
        P(None, "tensor"),
        P(None, "tensor"),
        P(),
    )
    return jax.shard_map(shards, mesh=mesh, in_specs=in_specs, out_specs=out_specs, check_vma=False)
```

profile of v0, /device:TPU:0, one launch (start us, length us, event | category | flops | bytes accessed | tf_op | source)
XLA Modules:
  0.0 445.8 jit_solution(11076342188607111506)
XLA Ops:
  0.6 1.3 select_maximum_fusion.refs_11_.refs_14_.refs_17_
  2.0 0.9 copy.36
  2.9 0.9 pad.8.refs_2_.refs_5_
  3.8 88.6 %forward.2 = (bf16[1536,1024]{1,0:T(8,128)(2,1)}, f32[1024,1]{1,0:T(8,128)}, f32[1024,384]{1,0:T(8,128)}, f32[1024,768]{1,0:T(8,128)}, f32[1024,768]{1,0:T(8,128...) custom-call(bf16[1024,1536]{1,0:T(8,128)(2,1)} %refs_9_.5, ...), custom_call_target="tpu_custom_call" | custom-call | tf_op jit(solution)/shard_map/forward/pallas_call | solution.py:839
  92.4 88.2 %forward.3 = (f32[1024,1536]{1,0:T(8,128)}, f32[8,1,128]{2,1,0:T(1,128)}, bf16[1536,1024]{1,0:T(8,128)(2,1)}, f32[1024,1]{1,0:T(8,128)}, f32[1024,384]{1,0:T(8,1...) custom-call(bf16[1024,1536]{1,0:T(8,128)(2,1)} %refs_9_.5, ...), custom_call_target="tpu_custom_call" | custom-call | tf_op jit(solution)/shard_map/forward/pallas_call | solution.py:839
  180.7 96.3 %back.2 = (f32[1024,1536]{1,0:T(8,128)}, f32[2,192,768]{2,1,0:T(8,128)}, bf16[8,192,768]{2,1,0:T(8,128)(2,1)}, bf16[1024,256]{1,0:T(8,128)(2,1)}, bf16[1024,128]...) custom-call(bf16[1024,1536]{1,0:T(8,128)(2,1)} %refs_0_.5, ...), custom_call_target="tpu_custom_call" | custom-call | tf_op jit(solution)/shard_map/back/pallas_call | solution.py:1398
  277.0 154.0 %back.3 = (f32[1024,1536]{1,0:T(8,128)}, f32[4,192,768]{2,1,0:T(8,128)}, bf16[2,8,80,256]{3,2,1,0:T(8,128)(2,1)}, bf16[4,2,400,256]{3,2,1,0:T(8,128)(2,1)}) custom-call(f32[1024,1536]{1,0:T(8,128)} %get-tuple-element.83.refs_0_, f32[8,1,128]{2,1,0:T(1,128)} %get-tuple-element.84.refs_1_, f32[1024,768]{1,0:T(8,128)} %get-tuple-element.85.refs_2_, ...), custom_call_target="tpu_custom_call" | custom-call | tf_op jit(solution)/shard_map/back/pallas_call | solution.py:1398
  431.0 12.9 %results.1 = (f32[2,16,1536]{2,1,0:T(8,128)}, f32[2,1536,256]{2,1,0:T(8,128)}, f32[2,4,768]{2,1,0:T(4,128)}, f32[2,768]{1,0:T(2,128)}, f32[2,4,256]{2,1,0:T(4,12...) custom-call(bf16[2,8,80,256]{3,2,1,0:T(8,128)(2,1)} %get-tuple-eleme, ...), custom_call_target="tpu_custom_call" | custom-call | tf_op jit(solution)/shard_map/results/pallas_call | solution.py:1477
  443.8 0.9 slice_bitcast_fusion
  444.8 0.8 copy.34
where the time goes:
time: 452 us; the launch traced here: 446 us
  Pallas kernels  440 us (97%)
    pallas_call x2, Pallas kernels, back(): pl.pallas_call(functools.partial(back_body, heads=heads, per=LEN // CHUNK...  250 us
    pallas_call x2, Pallas kernels, forward(): pl.pallas_call(functools.partial(forward_body, size=size, heads=heads, pe...  177 us
    pallas_call x1, Pallas kernels, write_results(): pl.pallas_call(functools.partial(results_body, layers=layers, heads=heads...  12.9 us

commit v1 on v0

--- a/solution.py
+++ b/solution.py
@@ -669,14 +669,19 @@
             tick()
 
         if mid:
+            job.relay(2, 1)
             project(0, inner)
             flush(2).start()
+            job.relay(2, 2)
         job.arrive(1)
         project(1, gate)
         flush(3).start()
-
-    for k in range(1, line.n):
-        @pl.when(i == 1 + (k - 1) * steps // line.n)
+        if not mid:
+            job.relay(2, 1)
+
+    passed = 2 if mid else 1
+    for k in range(passed + 1, line.n):
+        @pl.when(i == 1 + (k - passed - 1) * steps // line.n)
         def _(k=k):
             job.relay(2, k)
 
@@ -1189,7 +1194,7 @@
             job.product(held, turned, ilow)
             move(4).start()
         else:
-            job.emit(2, turned, ilow, places // 2)
+            job.emit(2, turned, ilow, places - 1)
             for k in (4, 5, 6):
                 move(k).start()
 
@@ -1243,8 +1248,6 @@
                 buffers[0].at[0], square.me, turned, step_all, sd_all, dcp_ref[...], dsp_ref[...], dhp_ref[...], dgain_ref[...]
             )
             minis.sum.start(0)
-            for m in range(places // 2, places - 1):
-                job.lead(2, m)
             for m in range(places // 2):
                 job.fold(2, m)
             finish(3)
@@ -1421,6 +1424,17 @@
     ]
     for copy in loads:
         copy.start()
+    moves = [
+        (up, up_out), (mixed, mixed_out), (first.at[pl.ds(1, 2)], pair_out.at[0]), (second.at[1], pair_out.at[1, 0]),
+        (first.at[3], pair_out.at[1, 1]), (first.at[0], out_out.at[0]), (second.at[0], out_out.at[1]),
+    ]
+    stores = [pltpu.make_async_copy(src, dst, store.at[k]) for k, (src, dst) in enumerate(moves)]
+    for k, copy in enumerate(stores):
+        if k < 3:
+            loads[k].wait()
+        if k == 3:
+            loads[3].wait()
+        copy.start()
     step_ref, state_ref, conv_ref, bias_ref, convs_ref, biass_ref = refs[:6]
     stepbias_ref, decay_ref, skip_ref, norm_ref, gain_ref = refs[6:]
     model = state_ref.shape[1]
@@ -1451,15 +1465,6 @@
         at += 8
         for b in range(model // w):
             gain_ref[layer : layer + 1, b * w : (b + 1) * w] = flat[at + b : at + b + 1]
-    for copy in loads:
-        copy.wait()
-    moves = [
-        (up, up_out), (mixed, mixed_out), (first.at[pl.ds(1, 2)], pair_out.at[0]), (second.at[1], pair_out.at[1, 0]),
-        (first.at[3], pair_out.at[1, 1]), (first.at[0], out_out.at[0]), (second.at[0], out_out.at[1]),
-    ]
-    stores = [pltpu.make_async_copy(src, dst, store.at[k]) for k, (src, dst) in enumerate(moves)]
-    for copy in stores:
-        copy.start()
     for copy in stores:
         copy.wait()
 

time: 452 us -> 458 us (1.013)
  Pallas kernels: 440 us -> 448 us
    pallas_call x2, Pallas kernels: 177 us -> 185 us  [forward(): pl.pallas_call(functools.partial(forward_body, size=size, heads=heads, pe...]
where the time goes in v1:
time: 458 us; the launch traced here: 454 us
  Pallas kernels  448 us (98%)
    pallas_call x2, Pallas kernels, back(): pl.pallas_call(functools.partial(back_body, heads=heads, per=LEN // CHUNK...  251 us
    pallas_call x2, Pallas kernels, forward(): pl.pallas_call(functools.partial(forward_body, size=size, heads=heads, pe...  185 us
    pallas_call x1, Pallas kernels, write_results(): pl.pallas_call(functools.partial(results_body, layers=layers, heads=heads...  11.8 us

profile of v1, /device:TPU:0, one launch (start us, length us, event | category | flops | bytes accessed | tf_op | source)
XLA Modules:
  0.0 453.6 jit_solution(4555413466786175385)
XLA Ops:
  0.6 1.3 select_maximum_fusion.refs_11_.refs_14_.refs_17_
  2.0 0.9 copy.36
  2.9 0.9 pad.8.refs_2_.refs_5_
  3.8 90.3 %forward.2 = (bf16[1536,1024]{1,0:T(8,128)(2,1)}, f32[1024,1]{1,0:T(8,128)}, f32[1024,384]{1,0:T(8,128)}, f32[1024,768]{1,0:T(8,128)}, f32[1024,768]{1,0:T(8,128...) custom-call(bf16[1024,1536]{1,0:T(8,128)(2,1)} %refs_9_.5, ...), custom_call_target="tpu_custom_call" | custom-call | tf_op jit(solution)/shard_map/forward/pallas_call | solution.py:844
  94.1 94.8 %forward.3 = (f32[1024,1536]{1,0:T(8,128)}, f32[8,1,128]{2,1,0:T(1,128)}, bf16[1536,1024]{1,0:T(8,128)(2,1)}, f32[1024,1]{1,0:T(8,128)}, f32[1024,384]{1,0:T(8,1...) custom-call(bf16[1024,1536]{1,0:T(8,128)(2,1)} %refs_9_.5, ...), custom_call_target="tpu_custom_call" | custom-call | tf_op jit(solution)/shard_map/forward/pallas_call | solution.py:844
  188.9 96.5 %back.2 = (f32[1024,1536]{1,0:T(8,128)}, f32[2,192,768]{2,1,0:T(8,128)}, bf16[8,192,768]{2,1,0:T(8,128)(2,1)}, bf16[1024,256]{1,0:T(8,128)(2,1)}, bf16[1024,128]...) custom-call(bf16[1024,1536]{1,0:T(8,128)(2,1)} %refs_0_.5, ...), custom_call_target="tpu_custom_call" | custom-call | tf_op jit(solution)/shard_map/back/pallas_call | solution.py:1401
  285.4 154.5 %back.3 = (f32[1024,1536]{1,0:T(8,128)}, f32[4,192,768]{2,1,0:T(8,128)}, bf16[2,8,80,256]{3,2,1,0:T(8,128)(2,1)}, bf16[4,2,400,256]{3,2,1,0:T(8,128)(2,1)}) custom-call(f32[1024,1536]{1,0:T(8,128)} %get-tuple-element.83.refs_0_, f32[8,1,128]{2,1,0:T(1,128)} %get-tuple-element.84.refs_1_, f32[1024,768]{1,0:T(8,128)} %get-tuple-element.85.refs_2_, ...), custom_call_target="tpu_custom_call" | custom-call | tf_op jit(solution)/shard_map/back/pallas_call | solution.py:1401
  439.9 11.8 %results.1 = (f32[2,16,1536]{2,1,0:T(8,128)}, f32[2,1536,256]{2,1,0:T(8,128)}, f32[2,4,768]{2,1,0:T(4,128)}, f32[2,768]{1,0:T(2,128)}, f32[2,4,256]{2,1,0:T(4,12...) custom-call(bf16[2,8,80,256]{3,2,1,0:T(8,128)(2,1)} %get-tuple-eleme, ...), custom_call_target="tpu_custom_call" | custom-call | tf_op jit(solution)/shard_map/results/pallas_call | solution.py:1482
  451.7 0.9 slice_bitcast_fusion
  452.6 0.8 copy.34

commit v2 on v1

--- a/solution.py
+++ b/solution.py
@@ -669,19 +669,14 @@
             tick()
 
         if mid:
-            job.relay(2, 1)
             project(0, inner)
             flush(2).start()
-            job.relay(2, 2)
         job.arrive(1)
         project(1, gate)
         flush(3).start()
-        if not mid:
-            job.relay(2, 1)
-
-    passed = 2 if mid else 1
-    for k in range(passed + 1, line.n):
-        @pl.when(i == 1 + (k - passed - 1) * steps // line.n)
+
+    for k in range(1, line.n):
+        @pl.when(i == 1 + k * steps // (line.n + 1))
         def _(k=k):
             job.relay(2, k)
 
@@ -928,12 +923,12 @@
 
     middle = begin_scan + steps // 2
     if last:
-        folds = [(spaced(begin_scan, middle, m), 0, m) for m in range(places)]
-        folds += [(spaced(middle, begin_norm, m) + 1, 1, m) for m in range(places)]
+        folds = [(spaced(begin_scan, middle, m) + 1, 0, m) for m in range(places)]
+        folds += [(spaced(middle, begin_norm, m) + 2, 1, m) for m in range(places)]
     else:
-        folds = [(spaced(begin_gate - 1, begin_scan + 3, m), 3, m) for m in range(places)]
-        folds += [(spaced(begin_scan + 2, middle + 3, m), 0, m) for m in range(places)]
-        folds += [(spaced(begin_norm - 1, end - 1, m), 1, m) for m in range(places)]
+        folds = [(spaced(begin_gate, begin_scan + 4, m), 3, m) for m in range(places)]
+        folds += [(spaced(begin_scan + 3, begin_norm + 1, m), 0, m) for m in range(places)]
+        folds += [(spaced(begin_norm, end, m), 1, m) for m in range(places)]
 
     def column(row):
         return jnp.broadcast_to(row, (n, n)).T[:, 0:1]
@@ -1194,7 +1189,7 @@
             job.product(held, turned, ilow)
             move(4).start()
         else:
-            job.emit(2, turned, ilow, places - 1)
+            job.emit(2, turned, ilow, places // 2)
             for k in (4, 5, 6):
                 move(k).start()
 
@@ -1248,6 +1243,8 @@
                 buffers[0].at[0], square.me, turned, step_all, sd_all, dcp_ref[...], dsp_ref[...], dhp_ref[...], dgain_ref[...]
             )
             minis.sum.start(0)
+            for m in range(places // 2, places - 1):
+                job.lead(2, m)
             for m in range(places // 2):
                 job.fold(2, m)
             finish(3)

time: 458 us -> 452 us (0.987)
  Pallas kernels: 448 us -> 441 us
    pallas_call x2, Pallas kernels: 185 us -> 177 us  [forward(): pl.pallas_call(functools.partial(forward_body, size=size, heads=heads, pe...]
where the time goes in v2:
time: 452 us; the launch traced here: 447 us
  Pallas kernels  441 us (98%)
    pallas_call x2, Pallas kernels, back(): pl.pallas_call(functools.partial(back_body, heads=heads, per=LEN // CHUNK...  252 us
    pallas_call x2, Pallas kernels, forward(): pl.pallas_call(functools.partial(forward_body, size=size, heads=heads, pe...  177 us
    pallas_call x1, Pallas kernels, write_results(): pl.pallas_call(functools.partial(results_body, layers=layers, heads=heads...  11.8 us

profile of v2, /device:TPU:0, one launch (start us, length us, event | category | flops | bytes accessed | tf_op | source)
XLA Modules:
  0.0 447.0 jit_solution(8430943629311650821)
XLA Ops:
  0.6 1.3 select_maximum_fusion.refs_11_.refs_14_.refs_17_
  2.0 0.9 copy.36
  2.9 0.9 pad.8.refs_2_.refs_5_
  3.8 87.4 %forward.2 = (bf16[1536,1024]{1,0:T(8,128)(2,1)}, f32[1024,1]{1,0:T(8,128)}, f32[1024,384]{1,0:T(8,128)}, f32[1024,768]{1,0:T(8,128)}, f32[1024,768]{1,0:T(8,128...) custom-call(bf16[1024,1536]{1,0:T(8,128)(2,1)} %refs_9_.5, ...), custom_call_target="tpu_custom_call" | custom-call | tf_op jit(solution)/shard_map/forward/pallas_call | solution.py:839
  91.2 90.0 %forward.3 = (f32[1024,1536]{1,0:T(8,128)}, f32[8,1,128]{2,1,0:T(1,128)}, bf16[1536,1024]{1,0:T(8,128)(2,1)}, f32[1024,1]{1,0:T(8,128)}, f32[1024,384]{1,0:T(8,1...) custom-call(bf16[1024,1536]{1,0:T(8,128)(2,1)} %refs_9_.5, ...), custom_call_target="tpu_custom_call" | custom-call | tf_op jit(solution)/shard_map/forward/pallas_call | solution.py:839
  181.2 97.1 %back.2 = (f32[1024,1536]{1,0:T(8,128)}, f32[2,192,768]{2,1,0:T(8,128)}, bf16[8,192,768]{2,1,0:T(8,128)(2,1)}, bf16[1024,256]{1,0:T(8,128)(2,1)}, bf16[1024,128]...) custom-call(bf16[1024,1536]{1,0:T(8,128)(2,1)} %refs_0_.5, ...), custom_call_target="tpu_custom_call" | custom-call | tf_op jit(solution)/shard_map/back/pallas_call | solution.py:1398
  278.3 155.0 %back.3 = (f32[1024,1536]{1,0:T(8,128)}, f32[4,192,768]{2,1,0:T(8,128)}, bf16[2,8,80,256]{3,2,1,0:T(8,128)(2,1)}, bf16[4,2,400,256]{3,2,1,0:T(8,128)(2,1)}) custom-call(f32[1024,1536]{1,0:T(8,128)} %get-tuple-element.83.refs_0_, f32[8,1,128]{2,1,0:T(1,128)} %get-tuple-element.84.refs_1_, f32[1024,768]{1,0:T(8,128)} %get-tuple-element.85.refs_2_, ...), custom_call_target="tpu_custom_call" | custom-call | tf_op jit(solution)/shard_map/back/pallas_call | solution.py:1398
  433.3 11.8 %results.1 = (f32[2,16,1536]{2,1,0:T(8,128)}, f32[2,1536,256]{2,1,0:T(8,128)}, f32[2,4,768]{2,1,0:T(4,128)}, f32[2,768]{1,0:T(2,128)}, f32[2,4,256]{2,1,0:T(4,12...) custom-call(bf16[2,8,80,256]{3,2,1,0:T(8,128)(2,1)} %get-tuple-eleme, ...), custom_call_target="tpu_custom_call" | custom-call | tf_op jit(solution)/shard_map/results/pallas_call | solution.py:1479
  445.1 0.9 slice_bitcast_fusion
  446.1 0.8 copy.34
